TPU v7x, 128 devices: a whole 4x4x4 slice. The times are simulated.
128 devices in a mesh: cell: 16 (over y, x), gene: 8 (over z, core).
Axes of the slice: x: 4, y: 4, z: 4, core: 2. Of those that a mesh axis runs over, the one named last changes fastest.
Arguments:
- expression: float32 [24576, 32768], P('cell', 'gene'), may hold values from -16 to 18, as said below
- tile_mask: int32 [96, 128], P('cell', 'gene'), may hold values from 0 to 1, as said below
- start: float32 [32768, 32], P('gene'), may hold values from -6 to 6
Outputs:
- alphas: float32 [2, 32, 32], replicated
- betas: float32 [2, 32, 32], replicated
- next_block: float32 [32768, 32], P('gene')
Inputs may be any that keep to these rules, and one draw needn't show every extreme that they name: expression: positive mean per gene with gene and cell scales and independent noise. `tile_mask`: each row of tiles belongs to one of 8 cell types and each column of tiles to one of 8 gene modules; a tile is 1 where its type expresses its module.
All inputs are finite; a program needn't handle non-finite values.
Results may differ from a plain program's by a relative error of at most 0.0024.
Values sent between devices are 32-bit elements; how exact they have to be, the bound alone decides.
A program may use at most 128 MiB of HBM per device.

v0:
```python
import math
import jax
import jax.numpy as jnp
from jax import lax
from jax.sharding import PartitionSpec as P

TILE = 256
STEPS = 2
highest = lax.Precision.HIGHEST


def transposed_dot(left, right):
    return lax.dot_general(
        left, right, (((0,), (0,)), ((), ())), precision=highest, preferred_element_type=jnp.float32
    )


def product(left, right):
    return jnp.dot(left, right, precision=highest, preferred_element_type=jnp.float32)


def finish(resid, gram):
    lower = jnp.linalg.cholesky(gram)
    fresh = lax.linalg.triangular_solve(lower, resid, left_side=False, lower=True, transpose_a=True)
    return (fresh, jnp.transpose(lower))


def expand_mask(expression, tile_mask):
    rows, width = expression.shape
    tiles = expression.reshape(tile_mask.shape[0], TILE, tile_mask.shape[1], TILE)
    return (tiles * tile_mask.astype(jnp.float32)[:, None, :, None]).reshape(rows, width)


def orthogonalize(image, current, older):
    projections = [transposed_dot(current, image)]
    if older is not None:
        projections.append(transposed_dot(older, image))
    summed = lax.psum(jnp.stack(projections), "gene")
    resid = image - product(current, summed[0])
    if older is not None:
        resid = resid - product(older, summed[1])
    gram = lax.psum(transposed_dot(resid, resid), "gene")
    fresh, beta = finish(resid, gram)
    return (fresh, summed[0], beta)


def per_device(expression, tile_mask, start):
    cell_count = lax.axis_size("cell")
    gene_count = lax.axis_size("gene")
    rows, width = expression.shape
    cells = rows * cell_count
    masked = expand_mask(expression, tile_mask)
    means = lax.psum(jnp.sum(masked, axis=0), "cell") / cells
    current = start
    gram_start = lax.psum(transposed_dot(current, current), "gene")
    current = finish(current, gram_start)[0]
    older = None
    alpha_list = []
    beta_list = []
    for step in range(STEPS):
        partial_side = product(masked, current) - product(means[None, :], current)
        cell_side = lax.psum(partial_side, "gene")
        image = lax.psum(transposed_dot(masked, cell_side) / cells, "cell")
        fresh, alpha, beta = orthogonalize(image, current, older)
        alpha_list.append(alpha)
        beta_list.append(beta)
        older = current
        current = fresh
    next_block = current * math.sqrt(width * gene_count)
    return (jnp.stack(alpha_list), jnp.stack(beta_list), next_block)


def solution(mesh):
    in_specs = (P("cell", "gene"), P("cell", "gene"), P("gene", None))
    out_specs = (P(), P(), P("gene", None))
    return jax.shard_map(
        per_device, mesh=mesh, in_specs=in_specs, out_specs=out_specs, check_vma=False
    )
```

profile of v0, /device:TPU:0, one launch (start us, length us, event | category | flops | bytes accessed | tf_op | source)
XLA Modules:
  0.0 673.6 jit_solution(17267883612236582695)
XLA Ops:
  7.2 0.7 convert_element_type.3
  8.0 0.3 copy-done
  8.2 0.6 fusion.14
  8.8 27.0 %psum.70 = f32[32,32]{0,1:T(8,128)S(1)} all-reduce(f32[32,32]{0,1:T(8,128)S(1)} %fusion.14), channel_id=1, replica_groups=mesh['cell'=16,'gene'=8] {'gene'}, use_global_device_ids=true, to_apply=%region_0.0 | all-reduce | flops 1024 | bytes 8192 | tf_op jit(solution)/shard_map/psum | solution.py:55
  35.9 2.9 cholesky.59
  38.8 0.6 compare_reduce_fusion.2
  39.4 0.7 fusion.1
  40.1 2.4 custom-call.7
  42.5 0.6 convolution_bitcast_fusion.2
  43.2 11.6 %mul.17 = f32[6,256,16,256]{3,2,1,0:T(8,128)} broadcast(f32[6,16]{1,0:T(8,128)S(1)} %convert_element_type.3), dimensions={0,2} | broadcast | bytes 25166208 | tf_op jit(solution)/shard_map/mul | solution.py:31
  54.8 27.6 %copy.16 = f32[192,8,16,256]{3,1,2,0:T(8,128)S(1)} copy(f32[192,8,16,256]{3,2,1,0:T(8,128)} %bitcast.98) | data formatting | bytes 50331648
  82.4 18.8 %fusion.13 = (f32[4096]{0:T(1024)S(1)}, f32[1536,4096]{1,0:T(8,128)}) fusion(f32[1536,4096]{1,0:T(8,128)} %param.6, f32[1536,4096]{1,0:T(8,128)S(1)} %bitcast.97), kind=kLoop, calls=%fused_computation.49 | loop fusion | flops 12578816 | bytes 75513856 | tf_op jit(solution)/shard_map/reduce_sum | solution.py:53
  101.1 74.6 %psum.71 = f32[4096]{0:T(1024)S(1)} all-reduce(f32[4096]{0:T(1024)S(1)} %get-tuple-element.8), channel_id=1, replica_groups=mesh['cell'=16,'gene'=8] {'cell'}, use_global_device_ids=true, to_apply=%region_4.7 | all-reduce | flops 4096 | bytes 32768 | tf_op jit(solution)/shard_map/psum | solution.py:53
  175.7 0.5 convolution_bitcast_fusion.7
  176.3 23.5 %convolution_subtract_fusion.4 = f32[1536,32]{1,0:T(8,128)} fusion(f32[1536,4096]{1,0:T(8,128)} %get-tuple-element.9, f32[4096,32]{0,1:T(8,128)S(1)} %convolution_bitcast_fusion.2, f32[32]{0:T(128)S(1)} %convolution_bitcast_fusion.7), kind=kOutput, calls=%fused_computation.10 | convolution fusion | flops 2415968256 | bytes 25886848 | tf_op jit(solution)/shard_map/dot_general | solution.py:19
  199.9 55.4 %all-reduce.5.cloned.1.call-done = f32[1536,32]{1,0:T(8,128)} async-done(((f32[1536,32]{1,0:T(8,128)}), f32[1536,32]{1,0:T(8,128)}) %all-reduce.5.cloned.1.call-update) | async-done | bytes 196624 | tf_op jit(solution)/shard_map/psum | solution.py:62
  255.3 18.8 %convolution_multiply_fusion.1 = f32[4096,32]{0,1:T(8,128)} fusion(f32[1536,4096]{1,0:T(8,128)} %get-tuple-element.9, f32[1536,32]{1,0:T(8,128)} %all-reduce.5.cloned.1.call-done), kind=kOutput, calls=%fused_computation.8 | convolution fusion | flops 2416050176 | bytes 25886720 | tf_op jit(solution)/shard_map/dot_general | solution.py:13
  274.2 84.2 %all-reduce.7.cloned.1.call-done = f32[4096,32]{0,1:T(8,128)} async-done(((f32[4096,32]{0,1:T(8,128)}), f32[4096,32]{0,1:T(8,128)}) %all-reduce.7.cloned.1.call-update) | async-done | bytes 524304 | tf_op jit(solution)/shard_map/psum | solution.py:63
  358.4 1.6 convolution_bitcast_fusion.5
  360.0 24.4 %psum.74 = f32[1,32,32]{2,1,0:T(8,128)S(1)} all-reduce(f32[1,32,32]{2,1,0:T(8,128)S(1)} %convolution_bitcast_fusion.5), channel_id=1, replica_groups=mesh['cell'=16,'gene'=8] {'gene'}, use_global_device_ids=true, to_apply=%region_7.10 | all-reduce | flops 1024 | bytes 8192 | tf_op jit(solution)/shard_map/psum | solution.py:38
  384.4 1.7 convolution_subtract_fusion.2
  386.0 0.6 fusion.15
  386.6 23.8 %psum.75 = f32[32,32]{0,1:T(8,128)S(1)} all-reduce(f32[32,32]{0,1:T(8,128)S(1)} %fusion.15), channel_id=1, replica_groups=mesh['cell'=16,'gene'=8] {'gene'}, use_global_device_ids=true, to_apply=%region_8.11 | all-reduce | flops 1024 | bytes 8192 | tf_op jit(solution)/shard_map/psum | solution.py:42
  410.5 2.9 cholesky.70
  413.4 0.6 compare_reduce_fusion.1
  414.1 0.7 fusion.10
  414.7 2.4 custom-call.8
  417.2 0.6 convolution_bitcast_fusion.1
  417.8 0.5 convolution_bitcast_fusion.6
  418.3 23.6 %convolution_subtract_fusion.3 = f32[1536,32]{1,0:T(8,128)} fusion(f32[1536,4096]{1,0:T(8,128)} %get-tuple-element.9, f32[4096,32]{0,1:T(8,128)S(1)} %convolution_bitcast_fusion.1, f32[32]{0:T(128)S(1)} %convolution_bitcast_fusion.6), kind=kOutput, calls=%fused_computation.9 | convolution fusion | flops 2415968256 | bytes 25886848 | tf_op jit(solution)/shard_map/dot_general | solution.py:19
  442.0 58.3 %all-reduce.9.cloned.1.call-done = f32[1536,32]{1,0:T(8,128)} async-done(((f32[1536,32]{1,0:T(8,128)}), f32[1536,32]{1,0:T(8,128)}) %all-reduce.9.cloned.1.call-update) | async-done | bytes 196624 | tf_op jit(solution)/shard_map/psum | solution.py:62
  500.3 18.8 %convolution_multiply_fusion = f32[4096,32]{0,1:T(8,128)} fusion(f32[1536,4096]{1,0:T(8,128)} %get-tuple-element.9, f32[1536,32]{1,0:T(8,128)} %all-reduce.9.cloned.1.call-done), kind=kOutput, calls=%fused_computation.7 | convolution fusion | flops 2416050176 | bytes 25886720 | tf_op jit(solution)/shard_map/dot_general | solution.py:13
  519.1 84.3 %all-reduce.11.cloned.1.call-done = f32[4096,32]{0,1:T(8,128)} async-done(((f32[4096,32]{0,1:T(8,128)}), f32[4096,32]{0,1:T(8,128)}) %all-reduce.11.cloned.1.call-update) | async-done | bytes 524304 | tf_op jit(solution)/shard_map/psum | solution.py:63
  603.4 1.6 convolution_bitcast_fusion.3
  605.0 1.6 convolution_bitcast_fusion.4
  606.6 24.5 %psum.78 = f32[2,32,32]{2,1,0:T(8,128)S(1)} all-reduce(f32[2,32,32]{2,1,0:T(8,128)S(1)} %pad_maximum_fusion), channel_id=1, replica_groups=mesh['cell'=16,'gene'=8] {'gene'}, use_global_device_ids=true, to_apply=%region_11.14 | all-reduce | flops 2048 | bytes 16384 | tf_op jit(solution)/shard_map/psum | solution.py:38
  631.1 1.7 convolution_subtract_fusion.1
  632.7 0.6 convolution_subtract_fusion
  633.4 0.6 pad_maximum_fusion.1
  634.0 0.6 fusion.16
  634.5 23.6 %psum.79 = f32[32,32]{0,1:T(8,128)S(1)} all-reduce(f32[32,32]{0,1:T(8,128)S(1)} %fusion.16), channel_id=1, replica_groups=mesh['cell'=16,'gene'=8] {'gene'}, use_global_device_ids=true, to_apply=%region_12.15 | all-reduce | flops 1024 | bytes 8192 | tf_op jit(solution)/shard_map/psum | solution.py:42
  658.1 0.1 copy.11
  658.2 2.9 cholesky.81
  661.1 0.6 compare_reduce_fusion
  661.8 0.7 select_bitcast_fusion
  662.4 2.4 custom-call.9
  664.9 1.4 fusion
  666.3 0.7 copy.12
  (23 shorter events, 0.5 us)
Async XLA Ops:
  7.2 1.1 copy-start
  7.2 248.1 %all-reduce.5.cloned.1.call-start = ((), (), s32[]{:S(2)}) async-start(), calls=%async_computation | async-start | bytes 1572864 | tf_op jit(solution)/shard_map/psum | solution.py:62
  199.8 158.6 %all-reduce.7.cloned.1.call-start = ((), (), s32[]{:S(2)}) async-start(), calls=%async_computation.1 | async-start | bytes 1048576 | tf_op jit(solution)/shard_map/psum | solution.py:63
  274.1 226.2 %all-reduce.9.cloned.1.call-start = ((), (), s32[]{:S(2)}) async-start(), calls=%async_computation.2 | async-start | bytes 1572864 | tf_op jit(solution)/shard_map/psum | solution.py:62
  418.3 248.7 %copy-start.1 = (f32[4096,32]{0,1:T(8,128)S(1)}, f32[4096,32]{0,1:T(8,128)}, u32[]{:S(2)}) copy-start(f32[4096,32]{0,1:T(8,128)} %param.8) | copy-start | bytes 1572868
  442.0 161.4 %all-reduce.11.cloned.1.call-start = ((), (), s32[]{:S(2)}) async-start(), calls=%async_computation.3 | async-start | bytes 1048576 | tf_op jit(solution)/shard_map/psum | solution.py:63
Sparse Core Ops, SparseCore 0:
  199.9 55.2 all-reduce.4
  274.2 84.0 all-reduce.6
  442.1 58.1 all-reduce.8
  519.2 84.0 all-reduce.10
where the time goes:
time: 674 us
  waiting for transfers between devices  282 us (42%)
  blocking collectives  198 us (29%)
  matrix products  98.9 us (15%)
  local copies, waits for them, and re-layouts  40.4 us (6%)
  other arithmetic  40.2 us (6%)
  between operations  13.9 us (2%)
    psum x2, waiting for transfers between devices, per_device(): image = lax.psum(transposed_dot(masked, cell_side) / cells, 'cell')  168 us
    psum x2, waiting for transfers between devices, per_device(): cell_side = lax.psum(partial_side, 'gene')  114 us
    psum x1, blocking collectives, per_device(): means = lax.psum(jnp.sum(masked, axis=0), 'cell') / cells  74.6 us
    dot_general x7, matrix products, product(): jnp.dot(left, right, precision=highest, preferred_element_type=jnp.float32)  52.1 us
    psum x2, blocking collectives, orthogonalize(): summed = lax.psum(jnp.stack(projections), 'gene')  48.9 us
    psum x2, blocking collectives, orthogonalize(): gram = lax.psum(transposed_dot(resid, resid), 'gene')  47.3 us
    dot_general x8, matrix products, transposed_dot(): lax.dot_general(left, right, (((0,), (0,)), ((), ())), precision=highest,...  44.1 us
    unnamed x6, local copies, waits for them, and re-layouts  28.6 us
  transfers between devices with their start and end apart: 4, of which 4 were waited for; matrix products, arithmetic and copies ran while one was open for 0% of the time, Pallas kernels for 0%

commit v1 on v0

--- a/solution.py
+++ b/solution.py
@@ -59,7 +59,11 @@
     beta_list = []
     for step in range(STEPS):
         partial_side = product(masked, current) - product(means[None, :], current)
-        cell_side = lax.psum(partial_side, "gene")
+        cell_side = partial_side
+        for hop in (1, 2, 4):
+            cell_side = cell_side + lax.ppermute(
+                cell_side, "gene", [(dev, dev ^ hop) for dev in range(8)]
+            )
         image = lax.psum(transposed_dot(masked, cell_side) / cells, "cell")
         fresh, alpha, beta = orthogonalize(image, current, older)
         alpha_list.append(alpha)

time: 674 us -> 601 us (0.89); the launches traced: 674 us -> 593 us
  waiting for transfers between devices: 282 us -> 192 us
  matrix products: 98.9 us -> 107 us
    psum x2 -> x0, waiting for transfers between devices: 114 us -> none  [per_device(): cell_side = lax.psum(partial_side, 'gene')]
    ppermute x0 -> x6, waiting for transfers between devices: none -> 31.9 us  [per_device(): lax.ppermute(cell_side, 'gene', [(dev, dev ^ hop) for dev in range(8)])]
    psum x2, waiting for transfers between devices: 168 us -> 160 us  [per_device(): image = lax.psum(transposed_dot(masked, cell_side) / cells, 'cell')]
  transfers between devices with their start and end apart: 4 -> 8, of which waited for: 4 -> 8; matrix products, arithmetic and copies ran while one was open for 0% -> 0% of each run, Pallas kernels for 0% -> 0%
where the time goes in v1:
time: 601 us; the launch traced here: 593 us
  blocking collectives  198 us (33%)
  waiting for transfers between devices  192 us (32%)
  matrix products  107 us (18%)
  local copies, waits for them, and re-layouts  40.4 us (7%)
  other arithmetic  40.3 us (7%)
  between operations  14.5 us (2%)
    psum x2, waiting for transfers between devices, per_device(): image = lax.psum(transposed_dot(masked, cell_side) / cells, 'cell')  160 us
    psum x1, blocking collectives, per_device(): means = lax.psum(jnp.sum(masked, axis=0), 'cell') / cells  75.1 us
    dot_general x7, matrix products, product(): jnp.dot(left, right, precision=highest, preferred_element_type=jnp.float32)  57.8 us
    psum x2, blocking collectives, orthogonalize(): summed = lax.psum(jnp.stack(projections), 'gene')  48.9 us
    psum x2, blocking collectives, orthogonalize(): gram = lax.psum(transposed_dot(resid, resid), 'gene')  47.1 us
    dot_general x8, matrix products, transposed_dot(): lax.dot_general(left, right, (((0,), (0,)), ((), ())), precision=highest,...  46.3 us
    ppermute x6, waiting for transfers between devices, per_device(): lax.ppermute(cell_side, 'gene', [(dev, dev ^ hop) for dev in range(8)])  31.9 us
    unnamed x6, local copies, waits for them, and re-layouts  28.6 us
  transfers between devices with their start and end apart: 8, of which 8 were waited for; matrix products, arithmetic and copies ran while one was open for 0% of the time, Pallas kernels for 0%

profile of v1, /device:TPU:0, one launch (start us, length us, event | category | flops | bytes accessed | tf_op | source)
XLA Modules:
  0.0 593.4 jit_solution(15973040228173182259)
XLA Ops:
  7.2 0.7 convert_element_type.3
  8.2 0.6 fusion.16
  8.8 27.0 %psum.56 = f32[32,32]{0,1:T(8,128)S(1)} all-reduce(f32[32,32]{0,1:T(8,128)S(1)} %fusion.16), channel_id=1, replica_groups=mesh['cell'=16,'gene'=8] {'gene'}, use_global_device_ids=true, to_apply=%region_0.0 | all-reduce | flops 1024 | bytes 8192 | tf_op jit(solution)/shard_map/psum | solution.py:55
  35.9 2.9 cholesky.59
  38.8 0.6 compare_reduce_fusion.2
  39.5 0.7 fusion.3
  40.1 2.4 custom-call.7
  42.5 0.6 convolution_bitcast_fusion.2
  43.2 11.6 %mul.17 = f32[6,256,16,256]{3,2,1,0:T(8,128)} broadcast(f32[6,16]{1,0:T(8,128)S(1)} %convert_element_type.3), dimensions={0,2} | broadcast | bytes 25166208 | tf_op jit(solution)/shard_map/mul | solution.py:31
  54.8 27.6 %copy.16 = f32[192,8,16,256]{3,1,2,0:T(8,128)S(1)} copy(f32[192,8,16,256]{3,2,1,0:T(8,128)} %bitcast.96) | data formatting | bytes 50331648
  82.4 18.8 %fusion.15 = (f32[4096]{0:T(1024)S(1)}, f32[1536,4096]{1,0:T(8,128)}) fusion(f32[1536,4096]{1,0:T(8,128)} %param.6, f32[1536,4096]{1,0:T(8,128)S(1)} %bitcast.95), kind=kLoop, calls=%fused_computation.51 | loop fusion | flops 12578816 | bytes 75513856 | tf_op jit(solution)/shard_map/reduce_sum | solution.py:53
  101.1 75.1 %psum.57 = f32[4096]{0:T(1024)S(1)} all-reduce(f32[4096]{0:T(1024)S(1)} %get-tuple-element.8), channel_id=1, replica_groups=mesh['cell'=16,'gene'=8] {'cell'}, use_global_device_ids=true, to_apply=%region_4.7 | all-reduce | flops 4096 | bytes 32768 | tf_op jit(solution)/shard_map/psum | solution.py:53
  176.8 26.4 %convolution_subtract_fusion.4 = f32[1536,32]{0,1:T(8,128)S(1)} fusion(f32[1536,4096]{1,0:T(8,128)} %get-tuple-element.9, f32[4096,32]{0,1:T(8,128)S(1)} %convolution_bitcast_fusion.2, f32[32]{0:T(128)S(1)} %convolution_bitcast_fusion.7), kind=kOutput, calls=%fused_computation.10 | convolution fusion | flops 2415968256 | bytes 25886848 | tf_op jit(solution)/shard_map/dot_general | solution.py:19
  203.3 1.4 collective-permute-done
  204.8 6.9 %collective-permute-done.1 = f32[1536,32]{0,1:T(8,128)S(1)} collective-permute-done((f32[1536,32]{0,1:T(8,128)S(1)}, f32[1536,32]{0,1:T(8,128)S(1)}, u32[]{:S(2)}, u32[]{:S(2)}) %collective-permute-start.1) | collective-permute-done | bytes 196640 | tf_op jit(solution)/shard_map/ppermute | solution.py:64
  211.9 7.6 %collective-permute-done.2 = f32[1536,32]{0,1:T(8,128)S(1)} collective-permute-done((f32[1536,32]{0,1:T(8,128)S(1)}, f32[1536,32]{0,1:T(8,128)S(1)}, u32[]{:S(2)}, u32[]{:S(2)}) %collective-permute-start.2) | collective-permute-done | bytes 196640 | tf_op jit(solution)/shard_map/ppermute | solution.py:64
  219.5 19.9 %convolution_multiply_fusion.1 = f32[4096,32]{0,1:T(8,128)} fusion(f32[1536,4096]{1,0:T(8,128)} %get-tuple-element.9, f32[1536,32]{0,1:T(8,128)S(1)} %add.43, f32[1536,32]{0,1:T(8,128)S(1)} %collective-permute-done.2), kind=kOutput, calls=%fused_computation.8 | convolution fusion | flops 2416099328 | bytes 26083328 | tf_op jit(solution)/shard_map/dot_general | solution.py:13
  239.7 78.7 %all-reduce.3.cloned.1.call-done = f32[4096,32]{0,1:T(8,128)} async-done(((f32[4096,32]{0,1:T(8,128)}), f32[4096,32]{0,1:T(8,128)}) %all-reduce.3.cloned.1.call-update) | async-done | bytes 524304 | tf_op jit(solution)/shard_map/psum | solution.py:67
  318.4 1.6 convolution_bitcast_fusion.5
  320.0 24.4 %psum.59 = f32[1,32,32]{2,1,0:T(8,128)S(1)} all-reduce(f32[1,32,32]{2,1,0:T(8,128)S(1)} %convolution_bitcast_fusion.5), channel_id=1, replica_groups=mesh['cell'=16,'gene'=8] {'gene'}, use_global_device_ids=true, to_apply=%region_6.9 | all-reduce | flops 1024 | bytes 8192 | tf_op jit(solution)/shard_map/psum | solution.py:38
  344.5 1.7 convolution_subtract_fusion.2
  346.1 0.6 fusion.17
  346.7 23.6 %psum.60 = f32[32,32]{0,1:T(8,128)S(1)} all-reduce(f32[32,32]{0,1:T(8,128)S(1)} %fusion.17), channel_id=1, replica_groups=mesh['cell'=16,'gene'=8] {'gene'}, use_global_device_ids=true, to_apply=%region_7.10 | all-reduce | flops 1024 | bytes 8192 | tf_op jit(solution)/shard_map/psum | solution.py:42
  370.3 2.9 cholesky.70
  373.3 0.6 compare_reduce_fusion.1
  373.9 0.7 fusion.12
  374.6 2.4 custom-call.8
  377.0 0.7 convolution_bitcast_fusion.1
  378.2 26.4 %convolution_subtract_fusion.3 = f32[1536,32]{0,1:T(8,128)S(1)} fusion(f32[1536,4096]{1,0:T(8,128)} %get-tuple-element.9, f32[4096,32]{0,1:T(8,128)S(1)} %convolution_bitcast_fusion.1, f32[32]{0:T(128)S(1)} %convolution_bitcast_fusion.6), kind=kOutput, calls=%fused_computation.9 | convolution fusion | flops 2415968256 | bytes 25886848 | tf_op jit(solution)/shard_map/dot_general | solution.py:19
  404.7 1.4 collective-permute-done.3
  406.3 6.9 %collective-permute-done.4 = f32[1536,32]{0,1:T(8,128)S(1)} collective-permute-done((f32[1536,32]{0,1:T(8,128)S(1)}, f32[1536,32]{0,1:T(8,128)S(1)}, u32[]{:S(2)}, u32[]{:S(2)}) %collective-permute-start.4) | collective-permute-done | bytes 196640 | tf_op jit(solution)/shard_map/ppermute | solution.py:64
  413.6 7.6 %collective-permute-done.5 = f32[1536,32]{0,1:T(8,128)S(1)} collective-permute-done((f32[1536,32]{0,1:T(8,128)S(1)}, f32[1536,32]{0,1:T(8,128)S(1)}, u32[]{:S(2)}, u32[]{:S(2)}) %collective-permute-start.5) | collective-permute-done | bytes 196640 | tf_op jit(solution)/shard_map/ppermute | solution.py:64
  421.2 20.0 %convolution_multiply_fusion = f32[4096,32]{0,1:T(8,128)} fusion(f32[1536,4096]{1,0:T(8,128)} %get-tuple-element.9, f32[1536,32]{0,1:T(8,128)S(1)} %add.46, f32[1536,32]{0,1:T(8,128)S(1)} %collective-permute-done.5), kind=kOutput, calls=%fused_computation.7 | convolution fusion | flops 2416099328 | bytes 26083328 | tf_op jit(solution)/shard_map/dot_general | solution.py:13
  441.1 81.5 %all-reduce.5.cloned.1.call-done = f32[4096,32]{0,1:T(8,128)} async-done(((f32[4096,32]{0,1:T(8,128)}), f32[4096,32]{0,1:T(8,128)}) %all-reduce.5.cloned.1.call-update) | async-done | bytes 524304 | tf_op jit(solution)/shard_map/psum | solution.py:67
  522.7 1.6 convolution_bitcast_fusion.3
  524.3 1.6 convolution_bitcast_fusion.4
  525.9 24.4 %psum.62 = f32[2,32,32]{2,1,0:T(8,128)S(1)} all-reduce(f32[2,32,32]{2,1,0:T(8,128)S(1)} %pad_maximum_fusion), channel_id=1, replica_groups=mesh['cell'=16,'gene'=8] {'gene'}, use_global_device_ids=true, to_apply=%region_9.12 | all-reduce | flops 2048 | bytes 16384 | tf_op jit(solution)/shard_map/psum | solution.py:38
  550.3 1.7 convolution_subtract_fusion.1
  552.0 0.6 convolution_subtract_fusion
  552.6 0.6 pad_maximum_fusion.1
  553.2 0.6 fusion.18
  553.8 23.6 %psum.63 = f32[32,32]{0,1:T(8,128)S(1)} all-reduce(f32[32,32]{0,1:T(8,128)S(1)} %fusion.18), channel_id=1, replica_groups=mesh['cell'=16,'gene'=8] {'gene'}, use_global_device_ids=true, to_apply=%region_10.13 | all-reduce | flops 1024 | bytes 8192 | tf_op jit(solution)/shard_map/psum | solution.py:42
  577.4 2.9 cholesky.81
  580.4 0.6 compare_reduce_fusion
  581.0 0.7 select_bitcast_fusion
  581.7 2.4 custom-call.9
  584.1 1.4 fusion
  585.6 0.7 copy.12
  (33 shorter events, 2.8 us)
Async XLA Ops:
  7.2 1.1 copy-start
  7.2 311.3 %all-reduce.3.cloned.1.call-start = ((), (), s32[]{:S(2)}) async-start(), calls=%async_computation | async-start | bytes 1048576 | tf_op jit(solution)/shard_map/psum | solution.py:67
  203.2 1.5 collective-permute-start
  204.8 7.0 %collective-permute-start.1 = (f32[1536,32]{0,1:T(8,128)S(1)}, f32[1536,32]{0,1:T(8,128)S(1)}, u32[]{:S(2)}, u32[]{:S(2)}) collective-permute-start(f32[1536,32]{0,1:T(8,128)S(1)} %add.42), channel_id=1, source_target_pairs={{0,2},{1,3},{2,0},{3,1},{4,6},{5,7},{6,4},{7,5},{8,10},{9,11},{10,... | collective-permute-start | bytes 589832 | tf_op jit(solution)/shard_map/ppermute | solution.py:64
  211.8 7.7 %collective-permute-start.2 = (f32[1536,32]{0,1:T(8,128)S(1)}, f32[1536,32]{0,1:T(8,128)S(1)}, u32[]{:S(2)}, u32[]{:S(2)}) collective-permute-start(f32[1536,32]{0,1:T(8,128)S(1)} %add.43), channel_id=1, source_target_pairs={{0,4},{1,5},{2,6},{3,7},{4,0},{5,1},{6,2},{7,3},{8,12},{9,13},{10,... | collective-permute-start | bytes 589832 | tf_op jit(solution)/shard_map/ppermute | solution.py:64
  239.5 283.2 %all-reduce.5.cloned.1.call-start = ((), (), s32[]{:S(2)}) async-start(), calls=%async_computation.1 | async-start | bytes 1048576 | tf_op jit(solution)/shard_map/psum | solution.py:67
  378.2 208.1 %copy-start.1 = (f32[4096,32]{0,1:T(8,128)S(1)}, f32[4096,32]{0,1:T(8,128)}, u32[]{:S(2)}) copy-start(f32[4096,32]{0,1:T(8,128)} %param.8) | copy-start | bytes 1572868
  404.6 1.5 collective-permute-start.3
  406.2 7.0 %collective-permute-start.4 = (f32[1536,32]{0,1:T(8,128)S(1)}, f32[1536,32]{0,1:T(8,128)S(1)}, u32[]{:S(2)}, u32[]{:S(2)}) collective-permute-start(f32[1536,32]{0,1:T(8,128)S(1)} %add.45), channel_id=1, source_target_pairs={{0,2},{1,3},{2,0},{3,1},{4,6},{5,7},{6,4},{7,5},{8,10},{9,11},{10,... | collective-permute-start | bytes 589832 | tf_op jit(solution)/shard_map/ppermute | solution.py:64
  413.2 7.9 %collective-permute-start.5 = (f32[1536,32]{0,1:T(8,128)S(1)}, f32[1536,32]{0,1:T(8,128)S(1)}, u32[]{:S(2)}, u32[]{:S(2)}) collective-permute-start(f32[1536,32]{0,1:T(8,128)S(1)} %add.46), channel_id=1, source_target_pairs={{0,4},{1,5},{2,6},{3,7},{4,0},{5,1},{6,2},{7,3},{8,12},{9,13},{10,... | collective-permute-start | bytes 589832 | tf_op jit(solution)/shard_map/ppermute | solution.py:64
Sparse Core Ops, SparseCore 0:
  239.6 78.7 all-reduce.2
  441.3 81.3 all-reduce.4
